TPU v7x, 32 devices: a whole 2x2x4 slice. The times are simulated.
32 devices in a mesh: tile: 2 (over x), gr: 4 (over y, core), gc: 4 (over z).
Axes of the slice: x: 2, y: 2, z: 4, core: 2. Of those that a mesh axis runs over, the one named last changes fastest.
Arguments:
- child_maps: float32 [2, 8, 1024, 1024], P('tile', None, 'gr', 'gc'), may hold values from -1.3 to 5
Outputs:
- merged: float32 [2, 8, 768, 1536], P('tile', None, 'gr', 'gc')
All inputs are finite; a program needn't handle non-finite values.
Results may differ from a plain program's by a relative error of at most 0.0001.
Values sent between devices are 32-bit elements; how exact they have to be, the bound alone decides.
A program may use at most 128 MiB of HBM per device.

v0:
```python
import jax
import jax.numpy as jnp
from jax import lax
from jax.sharding import PartitionSpec as P

EXTERIOR = 768
NEWTON = 4


def from_partner(x, axis, apart):
    return lax.ppermute(x, axis, [(i, i ^ 1 << apart) for i in range(lax.axis_size(axis))])


def product(left, right):
    return jnp.matmul(left, right, precision=lax.Precision.HIGHEST)


def on_device(child_maps):
    blocks = child_maps[0]
    merges = blocks.shape[0]
    block_size = blocks.shape[1]
    ext_count = EXTERIOR // 4
    int_count = block_size - ext_count
    ext_ext = blocks[:, :ext_count, :ext_count]
    ext_int = blocks[:, :ext_count, ext_count:]
    int_ext = blocks[:, ext_count:, :ext_count]
    int_int = blocks[:, ext_count:, ext_count:]
    sibling = from_partner(int_int, "tile", 0)
    pieces = lax.all_gather((int_int + sibling)[:, None], ("gr", "gc"), axis=1, tiled=True)
    row_groups = lax.axis_size("gr")
    col_groups = lax.axis_size("gc")
    iface_size = row_groups * int_count
    interface = pieces.reshape(merges, row_groups, col_groups, int_count, int_count)
    interface = interface.transpose(0, 1, 3, 2, 4).reshape(
        merges, iface_size, col_groups * int_count
    )
    largest = jnp.max(jnp.diagonal(interface, axis1=1, axis2=2), axis=1)
    identity = jnp.eye(iface_size, dtype=jnp.float32)
    inverse = identity[None] / largest[:, None, None]
    for newton_step in range(NEWTON):
        inverse = 2.0 * inverse - product(product(inverse, interface), inverse)
    ext_coupling = lax.all_gather(ext_int, "gc", axis=2, tiled=True)
    own_cols = lax.all_gather(int_ext, "gr", axis=1, tiled=True)
    own_solved = product(inverse, own_cols)
    other_solved = from_partner(own_solved, "tile", 0)
    even_tile = lax.axis_index("tile") % 2 == 0
    left_half = jnp.where(even_tile, own_solved, other_solved)
    second = jnp.where(even_tile, other_solved, own_solved)
    solved = jnp.stack([left_half, second], axis=2).reshape(merges, iface_size, 2 * ext_count)
    blank_part = jnp.zeros_like(ext_ext)
    exterior = jnp.where(
        even_tile,
        jnp.concatenate([ext_ext, blank_part], axis=-1),
        jnp.concatenate([blank_part, ext_ext], axis=-1),
    )
    merged = exterior - product(ext_coupling, solved)
    return merged[None]


def solution(mesh):
    in_specs = (P("tile", None, "gr", "gc"),)
    out_specs = P("tile", None, "gr", "gc")
    return jax.shard_map(
        on_device, mesh=mesh, in_specs=in_specs, out_specs=out_specs, check_vma=False
    )
```

profile of v0, /device:TPU:1, one launch (start us, length us, event | category | flops | bytes accessed | tf_op | source)
XLA Modules:
  0.0 181.4 jit_solution(5565883241502704390)
XLA Ops:
  6.5 1.1 slice.19
  7.6 2.1 %collective-permute-start = (f32[8,64,64]{2,1,0:T(8,128)S(1)}, f32[8,64,64]{2,1,0:T(8,128)S(1)}, u32[]{:S(2)}, u32[]{:S(2)}) collective-permute-start(f32[8,64,64]{2,1,0:T(8,128)S(1)} %slice.19), channel_id=1, source_target_pairs={{0,16},{16,0},{1,17},{17,1},{2,18},{18,2},{3,19},{19,3},{4,20},{20... | collective-permute-start | bytes 393224 | tf_op jit(solution)/shard_map/ppermute | solution.py:11
  9.7 6.0 %collective-permute-done = f32[8,64,64]{2,1,0:T(8,128)S(1)} collective-permute-done((f32[8,64,64]{2,1,0:T(8,128)S(1)}, f32[8,64,64]{2,1,0:T(8,128)S(1)}, u32[]{:S(2)}, u32[]{:S(2)}) %collective-permute-start) | collective-permute-done | bytes 131104 | tf_op jit(solution)/shard_map/ppermute | solution.py:11
  15.8 1.8 slice_add_fusion
  17.6 0.0 all-gather.5.cloned.1.call-start
  17.6 1.9 %slice.20 = f32[8,64,192]{2,1,0:T(8,128)} slice(f32[8,256,256]{2,1,0:T(8,128)} %bitcast.38), slice={[0:8], [192:256], [0:192]} | slice | bytes 786432 | tf_op jit(solution)/shard_map/slice | solution.py:26
  19.6 0.0 all-gather.7.cloned.1.call-start
  19.6 1.4 slice.21
  21.1 1.2 copy.11
  22.3 48.7 %all-gather.9.cloned.1.call-done = f32[8,1024,64]{2,1,0:T(8,128)} async-done(((f32[8,64,64]{2,1,0:T(8,128)}), f32[8,1024,64]{2,1,0:T(8,128)}) %all-gather.9.cloned.1.call-update) | async-done | bytes 2097168 | tf_op jit(solution)/shard_map/all_gather | solution.py:29
  71.0 7.8 %copy.20 = f32[8,4,4,64,64]{4,2,3,1,0:T(4,128)} copy(f32[8,4,4,64,64]{4,3,2,1,0:T(8,128)} %bitcast.41) | data formatting | bytes 4194304 | tf_op jit(solution)/shard_map/reshape | solution.py:33
  78.7 4.3 %reshape.19 = f32[8,256,256]{2,1,0:T(8,128)S(1)} reshape(f32[8,4,64,4,64]{4,3,2,1,0:T(4,128)} %bitcast.33) | data formatting | bytes 4194304 | tf_op jit(solution)/shard_map/reshape | solution.py:34
  83.0 16.6 %copy.9 = f32[8,256,256]{0,2,1:T(8,128)} copy(f32[8,256,256]{2,1,0:T(8,128)S(1)} %reshape.19) | data formatting | bytes 4194304 | tf_op jit(solution)/shard_map/reshape | solution.py:34
  99.5 2.4 %gather_fusion = f32[256,8]{1,0:T(8,128)S(1)} fusion(f32[8,256,256]{0,2,1:T(8,128)} %copy.9, s32[256]{0:T(256)S(1)} %bitcast.34), kind=kCustom, calls=%fused_computation | custom fusion | bytes 18432 | tf_op jit(solution)/shard_map/jit(diagonal)/gather | solution.py:37
  101.9 0.1 reduce_max.9
  102.0 2.2 %fusion.8 = f32[8,256,256]{2,1,0:T(8,128)S(1)} fusion(f32[8,256,256]{2,1,0:T(8,128)S(1)} %reshape.19, f32[8]{0:T(128)S(1)} %reduce_max.9, f32[256,256]{1,0:T(8,128)S(1)} %fusion.19), kind=kOutput, calls=%fused_computation.15 | convolution fusion | flops 1611137024 | bytes 4456480 | tf_op jit(solution)/shard_map/dot_general | solution.py:15
  104.2 2.5 %multiply_subtract_fusion.2 = f32[8,256,256]{2,1,0:T(8,128)S(1)} fusion(f32[8,256,256]{2,1,0:T(8,128)S(1)} %fusion.8, f32[8]{0:T(128)S(1)} %reduce_max.9, f32[256,256]{1,0:T(8,128)S(1)} %fusion.19), kind=kOutput, calls=%fused_computation.12 | convolution fusion | flops 1612709888 | bytes 4456480 | tf_op jit(solution)/shard_map/dot_general | solution.py:15
  106.7 2.2 %fusion.21 = f32[8,256,256]{2,1,0:T(8,128)S(1)} fusion(f32[8,256,256]{2,1,0:T(8,128)S(1)} %multiply_subtract_fusion.2, f32[8,256,256]{2,1,0:T(8,128)S(1)} %reshape.19), kind=kOutput, calls=%fused_computation.29 | convolution fusion | flops 1610612736 | bytes 6291456 | tf_op jit(solution)/shard_map/dot_general | solution.py:15
  108.9 2.3 %multiply_subtract_fusion.1 = f32[8,256,256]{2,1,0:T(8,128)S(1)} fusion(f32[8,256,256]{2,1,0:T(8,128)S(1)} %multiply_subtract_fusion.2, f32[8,256,256]{2,1,0:T(8,128)S(1)} %fusion.21), kind=kOutput, calls=%fused_computation.11 | convolution fusion | flops 1611661312 | bytes 6291456 | tf_op jit(solution)/shard_map/dot_general | solution.py:15
  111.2 2.4 %fusion.22 = f32[8,256,256]{2,1,0:T(8,128)S(1)} fusion(f32[8,256,256]{2,1,0:T(8,128)S(1)} %multiply_subtract_fusion.1, f32[8,256,256]{2,1,0:T(8,128)S(1)} %reshape.19), kind=kOutput, calls=%fused_computation.30 | convolution fusion | flops 1610612736 | bytes 6291456 | tf_op jit(solution)/shard_map/dot_general | solution.py:15
  113.7 2.3 %multiply_subtract_fusion = f32[8,256,256]{2,1,0:T(8,128)S(1)} fusion(f32[8,256,256]{2,1,0:T(8,128)S(1)} %multiply_subtract_fusion.1, f32[8,256,256]{2,1,0:T(8,128)S(1)} %fusion.22), kind=kOutput, calls=%fused_computation.10 | convolution fusion | flops 1611661312 | bytes 6291456 | tf_op jit(solution)/shard_map/dot_general | solution.py:15
  116.0 2.2 %fusion.23 = f32[8,256,256]{2,1,0:T(8,128)S(1)} fusion(f32[8,256,256]{2,1,0:T(8,128)S(1)} %multiply_subtract_fusion, f32[8,256,256]{2,1,0:T(8,128)S(1)} %reshape.19), kind=kOutput, calls=%fused_computation.31 | convolution fusion | flops 1610612736 | bytes 6291456 | tf_op jit(solution)/shard_map/dot_general | solution.py:15
  118.2 2.1 %fusion.24 = f32[8,256,256]{2,1,0:T(8,128)S(1)} fusion(f32[8,256,256]{2,1,0:T(8,128)S(1)} %fusion.23, f32[8,256,256]{2,1,0:T(8,128)S(1)} %multiply_subtract_fusion), kind=kOutput, calls=%fused_computation.32 | convolution fusion | flops 1610612736 | bytes 6291456 | tf_op jit(solution)/shard_map/dot_general | solution.py:15
  120.4 0.0 all-gather.5.cloned.1.call-done
  120.4 7.0 %fusion.3 = f32[8,256,192]{1,2,0:T(8,128)} fusion(f32[8,256,192]{2,1,0:T(8,128)} %all-gather.5.cloned.1.call-done, f32[8,256,256]{2,1,0:T(8,128)S(1)} %fusion.24, f32[8,256,256]{2,1,0:T(8,128)} %copy-done), kind=kOutput, calls=%fused_computation.7 | convolution fusion | flops 1209008128 | bytes 7340032 | tf_op jit(solution)/shard_map/dot_general | solution.py:15
  127.4 1.3 collective-permute-start.1
  128.7 2.7 %slice.18 = f32[8,192,192]{2,1,0:T(8,128)} slice(f32[8,256,256]{2,1,0:T(8,128)} %bitcast.40), slice={[0:8], [0:192], [0:192]} | slice | bytes 2359296 | tf_op jit(solution)/shard_map/slice | solution.py:24
  131.4 32.0 %collective-permute-done.1 = f32[8,256,192]{1,2,0:T(8,128)S(1)} collective-permute-done((f32[8,256,192]{1,2,0:T(8,128)}, f32[8,256,192]{1,2,0:T(8,128)S(1)}, u32[]{:S(2)}, u32[]{:S(2)}) %collective-permute-start.1) | collective-permute-done | bytes 1572896 | tf_op jit(solution)/shard_map/ppermute | solution.py:11
  163.4 1.7 select_bitcast_fusion.1
  165.1 0.3 pad_maximum_fusion
  165.4 0.3 copy.10
  165.7 9.2 %fusion = f32[1,8,192,384]{3,2,1,0:T(8,128)} fusion(f32[8,192,192]{2,1,0:T(8,128)} %slice.18, f32[8,256,384]{1,2,0:T(8,128)S(1)} %bitcast.35, f32[8,192,256]{1,0,2:T(8,128)} %all-gather.7.cloned.1.call-done, pred[]{:T(512)S(6)} %eq.12), kind=kOutput, calls=%fused_computation.4 | convolution fusion | flops 1813118976 | bytes 8257537 | tf_op jit(solution)/shard_map/dot_general | solution.py:15
  (9 shorter events, 0.1 us)
Async XLA Ops:
  6.5 64.4 %all-gather.9.cloned.1.call-start = ((), (), s32[]{:S(2)}) async-start(), calls=%async_computation.2 | async-start | bytes 4456448 | tf_op jit(solution)/shard_map/all_gather | solution.py:29
  7.6 8.1 %collective-permute-start = (f32[8,64,64]{2,1,0:T(8,128)S(1)}, f32[8,64,64]{2,1,0:T(8,128)S(1)}, u32[]{:S(2)}, u32[]{:S(2)}) collective-permute-start(f32[8,64,64]{2,1,0:T(8,128)S(1)} %slice.19), channel_id=1, source_target_pairs={{0,16},{16,0},{1,17},{17,1},{2,18},{18,2},{3,19},{19,3},{4,20},{20... | collective-permute-start | bytes 393224 | tf_op jit(solution)/shard_map/ppermute | solution.py:11
  17.6 102.8 %all-gather.5.cloned.1.call-start = ((), (), s32[]{:S(2)}) async-start(), calls=%async_computation | async-start | bytes 2621440 | tf_op jit(solution)/shard_map/all_gather | solution.py:43
  19.6 146.1 %all-gather.7.cloned.1.call-start = ((), (), s32[]{:S(2)}) async-start(), calls=%async_computation.1 | async-start | bytes 2621440 | tf_op jit(solution)/shard_map/all_gather | solution.py:42
  116.0 2.2 %copy-start = (f32[8,256,256]{2,1,0:T(8,128)}, f32[8,256,256]{2,1,0:T(8,128)S(1)}, u32[]{:S(2)}) copy-start(f32[8,256,256]{2,1,0:T(8,128)S(1)} %multiply_subtract_fusion) | copy-start | bytes 6291460
  127.4 36.0 %collective-permute-start.1 = (f32[8,256,192]{1,2,0:T(8,128)}, f32[8,256,192]{1,2,0:T(8,128)S(1)}, u32[]{:S(2)}, u32[]{:S(2)}) collective-permute-start(f32[8,256,192]{1,2,0:T(8,128)} %fusion.3), channel_id=1, source_target_pairs={{0,16},{16,0},{1,17},{17,1},{2,18},{18,2},{3,19},{19,3},{4,20},{20... | collective-permute-start | bytes 4718600 | tf_op jit(solution)/shard_map/ppermute | solution.py:11
Sparse Core Ops, SparseCore 0:
  17.7 53.1 all-gather.8
  72.5 21.0 all-gather.4
  95.2 45.5 all-gather.6
where the time goes:
time: 183 us; the launch traced here: 181 us
  waiting for transfers between devices  86.8 us (47%)
  local copies, waits for them, and re-layouts  39.5 us (22%)
  matrix products  34.5 us (19%)
  between operations  13.3 us (7%)
  other arithmetic  3.85 us (2%)
  starting transfers between devices  3.5 us (2%)
    all_gather x1, waiting for transfers between devices, on_device(): lax.all_gather((int_int + sibling)[:, None], ('gr', 'gc'), axis=1, tiled=...  48.7 us
    ppermute x2, waiting for transfers between devices, from_partner(): lax.ppermute(x, axis, [(i, i ^ 1 << apart) for i in range(lax.axis_size(a...  38.1 us
    dot_general x10, matrix products, product(): return jnp.matmul(left, right, precision=lax.Precision.HIGHEST)  34.5 us
    reshape x2, local copies, waits for them, and re-layouts, on_device(): interface.transpose(0, 1, 3, 2, 4)  20.8 us
    reshape x1, local copies, waits for them, and re-layouts, on_device(): pieces.reshape(merges, row_groups, col_groups, int_count, int_count)  7.75 us
  transfers between devices with their start and end apart: 5, of which 3 were waited for; matrix products, arithmetic and copies ran while one was open for 36% of the time, Pallas kernels for 0%

commit v1 on v0

v1 whole, which is shorter than its diff:
```python
import functools

import jax
import jax.numpy as jnp
from jax import lax
from jax.experimental import pallas as pl
from jax.experimental.pallas import tpu as pltpu
from jax.sharding import PartitionSpec as P

EXTERIOR = 768
NEWTON = 4
MESH = pl.DeviceIdType.MESH
CHUNKS = 4


def dot32(left, right):
    return jnp.dot(
        left, right, precision=lax.Precision.HIGHEST, preferred_element_type=jnp.float32
    )


def halves(x):
    high = x.astype(jnp.bfloat16)
    return high, (x - high.astype(jnp.float32)).astype(jnp.bfloat16)


def dot3(left, right):
    lh, ll = halves(left)
    rh, rl = halves(right)
    dot = functools.partial(jnp.dot, preferred_element_type=jnp.float32)
    return dot(lh, rh) + (dot(lh, rl) + dot(ll, rh))


def kernel(
    groups, x_ref, out_ref, rows, strips, ei, wall,
    row_send, row_recv, strip_send, strip_recv, ei_send, ei_recv, w_send, w_recv,
):
    merges, block, _ = x_ref.shape
    ext = EXTERIOR // 4
    num = block - ext
    half_ext = ext // 2
    per = merges // CHUNKS
    tile = lax.axis_index("tile")
    gr = lax.axis_index("gr")
    gc = lax.axis_index("gc")
    side = tile % 2
    core = gr % 2
    pos = gr // 2
    me = side * 4 + gr

    def across(j):
        far_side = 1 - side if j & 4 else side
        far_pos = 1 - pos if j & 2 else pos
        far_core = 1 - core if j & 1 else core
        device = {"tile": tile - side + far_side, "gr": far_pos * 2 + far_core}
        return device, far_side * 4 + far_pos * 2 + far_core

    barrier = pltpu.get_barrier_semaphore()
    for j in range(1, 8):
        pl.semaphore_signal(barrier, inc=1, device_id=across(j)[0], device_id_type=MESH)
    for d in range(1, groups):
        pl.semaphore_signal(
            barrier, inc=1, device_id={"gc": (gc + d) % groups}, device_id_type=MESH
        )
    pl.semaphore_wait(barrier, 7 + groups - 1)

    def row_copy(part, j):
        device, other = across(j)
        lanes = pl.ds(ext - num, 2 * num) if part == 0 else pl.ds(0, ext - num)
        return pltpu.make_async_remote_copy(
            src_ref=x_ref.at[other, pl.ds(ext, num), lanes],
            dst_ref=rows.at[part, me],
            send_sem=row_send.at[part, j - 1],
            recv_sem=row_recv.at[part, j - 1],
            device_id=device,
            device_id_type=MESH,
        )

    def ei_copy(way, d, k):
        source = gc - d if way == 0 else gc + d
        part = pl.ds(k * per, per)
        return pltpu.make_async_remote_copy(
            src_ref=ei.at[source, part],
            dst_ref=ei.at[source, part],
            send_sem=ei_send.at[way, d, k],
            recv_sem=ei_recv.at[way, d, k],
            device_id={"gc": gc + 1 if way == 0 else gc - 1},
            device_id_type=MESH,
        )

    def sends(way, d):
        if way == 0:
            return jnp.logical_and(gc < groups - 1, gc >= d)
        return jnp.logical_and(gc > 0, gc + d < groups)

    def gets(way, d):
        return gc - 1 - d >= 0 if way == 0 else gc + 1 + d < groups

    def ei_start(d, k):
        for way in range(2):
            @pl.when(sends(way, d))
            def _():
                ei_copy(way, d, k).start()

    def ei_get(d, k):
        for way in range(2):
            @pl.when(gets(way, d))
            def _():
                ei_copy(way, d, k).wait_recv()

    for j in range(1, 8):
        row_copy(0, j).start()
    rows[0, me] = x_ref[me, ext:, ext - num:]
    rows[1, me] = x_ref[me, ext:, : ext - num]

    def pack(m, carry):
        ei[gc, m] = jnp.concatenate(
            [x_ref[m, :half_ext, ext:], x_ref[m, half_ext:ext, ext:]], axis=1
        )
        return carry

    lax.fori_loop(0, merges, pack, 0)
    ei_start(0, 0)
    for j in range(1, 8):
        row_copy(1, j).start()

    for j in range(1, 8):
        row_copy(0, j).wait_recv()
    total = [rows[0, g][:, num:] + rows[0, 4 + g][:, num:] for g in range(4)]
    left = jnp.concatenate(total[:2], axis=0)
    right = jnp.concatenate(total[2:], axis=0)
    strips[gc] = jnp.concatenate([left, right], axis=1)

    def strip_copy(d):
        return pltpu.make_async_remote_copy(
            src_ref=strips.at[gc],
            dst_ref=strips.at[gc],
            send_sem=strip_send.at[d - 1],
            recv_sem=strip_recv.at[d - 1],
            device_id={"gc": (gc + d) % groups},
            device_id_type=MESH,
        )

    for d in range(1, groups):
        strip_copy(d).start()
    for k in range(1, CHUNKS):
        ei_start(0, k)

    for j in range(1, 8):
        row_copy(1, j).wait_recv()
    couplings = jnp.concatenate(
        [
            jnp.concatenate(
                [
                    jnp.concatenate([rows[1, s * 4 + g], rows[0, s * 4 + g][:, :num]], axis=1)
                    for s in range(2)
                ],
                axis=1,
            )
            for g in range(4)
        ],
        axis=0,
    )

    for d in range(1, groups):
        strip_copy(d).wait_recv()
    interface = jnp.concatenate(
        [
            jnp.concatenate([strips[g][:, :num] for g in range(groups)], axis=1),
            jnp.concatenate([strips[g][:, num:] for g in range(groups)], axis=1),
        ],
        axis=0,
    )
    eye = lax.broadcasted_iota(jnp.int32, interface.shape, 0) == lax.broadcasted_iota(
        jnp.int32, interface.shape, 1
    )
    largest = jnp.max(jnp.where(eye, interface, -jnp.inf), axis=(0, 1), keepdims=True)
    scale = 1.0 / largest
    inverse = jnp.where(eye, 2.0 * scale, 0.0) - (interface * scale) * scale
    for step in range(NEWTON - 1):
        inverse = 2.0 * inverse - dot32(dot32(inverse, interface), inverse)
        if step == NEWTON - 3:
            ei_get(0, 0)
            ei_start(1, 0)
    wall[me] = dot32(inverse, couplings)

    size = wall.shape[1] // 2

    def w_copy(index, owner, half, j):
        part = pl.ds(half * size, size)
        return pltpu.make_async_remote_copy(
            src_ref=wall.at[owner, part],
            dst_ref=wall.at[owner, part],
            send_sem=w_send.at[index],
            recv_sem=w_recv.at[index],
            device_id=across(j)[0],
            device_id_type=MESH,
        )

    own = me
    far = {j: across(j)[1] for j in (2, 4, 6)}
    moves = {}
    index = 0
    for half in range(2):
        for j in (4, 2, 1):
            moves["own", half, j] = w_copy(index, own, half, j)
            index += 1
        for j in (4, 2, 6):
            moves["pass", half, j] = w_copy(index, far[j], half, 1)
            index += 1
    moves["turn", 1, 4] = w_copy(index, far[4], 1, 2)
    moves["turn", 0, 2] = w_copy(index + 1, far[2], 0, 4)

    for half in (1, 0):
        for j in (4, 2) if half else (2, 4):
            moves["own", half, j].start()
    for half in (1, 0):
        moves["own", half, 1].start()
    for k in range(1, CHUNKS):
        ei_get(0, k)
        ei_start(1, k)
    moves["own", 1, 4].wait_recv()
    moves["turn", 1, 4].start()
    moves["pass", 1, 4].start()
    moves["own", 0, 2].wait_recv()
    moves["turn", 0, 2].start()
    moves["pass", 0, 2].start()
    for d in range(1, groups - 1):
        for k in range(CHUNKS):
            ei_get(d, k)
            if d + 1 < groups - 1:
                ei_start(d + 1, k)
        if d == 1:
            for half, j in ((1, 2), (0, 4)):
                moves["own", half, j].wait_recv()
                moves["pass", half, j].start()
            moves["turn", 1, 4].wait_recv()
            moves["pass", 1, 6].start()
            moves["turn", 0, 2].wait_recv()
            moves["pass", 0, 6].start()
    for half in range(2):
        moves["own", half, 1].wait_recv()
        for j in (4, 2, 6):
            moves["pass", half, j].wait_recv()

    def finish(m, carry):
        coupling = jnp.concatenate(
            [
                jnp.concatenate([ei[g, m][:, :num] for g in range(groups)], axis=1),
                jnp.concatenate([ei[g, m][:, num:] for g in range(groups)], axis=1),
            ],
            axis=0,
        )
        own_part = x_ref[m, :ext, :ext]
        blank = jnp.zeros_like(own_part)
        first = jnp.where(side == 0, own_part, blank)
        second = jnp.where(side == 0, blank, own_part)
        out_ref[m] = jnp.concatenate([first, second], axis=1) - dot3(coupling, wall[m])
        return carry

    lax.fori_loop(0, merges, finish, 0)

    for j in range(1, 8):
        for part in range(2):
            row_copy(part, j).wait_send()
    for d in range(1, groups):
        strip_copy(d).wait_send()
    for way in range(2):
        for d in range(groups - 1):
            @pl.when(sends(way, d))
            def _():
                for k in range(CHUNKS):
                    ei_copy(way, d, k).wait_send()
    for move in moves.values():
        move.wait_send()


def on_device(groups, child_maps):
    blocks = child_maps[0]
    merges, block, _ = blocks.shape
    ext = EXTERIOR // 4
    num = block - ext
    dma = pltpu.SemaphoreType.DMA
    f32 = jnp.float32
    merged = pl.pallas_call(
        functools.partial(kernel, groups),
        out_shape=jax.ShapeDtypeStruct((merges, ext, 2 * ext), f32),
        in_specs=[pl.BlockSpec(memory_space=pltpu.VMEM)],
        out_specs=pl.BlockSpec(memory_space=pltpu.VMEM),
        scratch_shapes=[
            pltpu.VMEM((2, merges, num, 2 * num), f32),
            pltpu.VMEM((groups, 2 * num, 2 * num), f32),
            pltpu.VMEM((groups, merges, ext // 2, 2 * num), f32),
            pltpu.VMEM((merges, 4 * num, 2 * ext), f32),
            dma((2, 7)),
            dma((2, 7)),
            dma((groups - 1,)),
            dma((groups - 1,)),
            dma((2, groups - 1, CHUNKS)),
            dma((2, groups - 1, CHUNKS)),
            dma((14,)),
            dma((14,)),
        ],
        compiler_params=pltpu.CompilerParams(
            collective_id=0, has_side_effects=True, vmem_limit_bytes=48 * 1024 * 1024
        ),
    )(blocks)
    return merged[None]


def solution(mesh):
    in_specs = (P("tile", None, "gr", "gc"),)
    out_specs = P("tile", None, "gr", "gc")
    return jax.shard_map(
        functools.partial(on_device, mesh.shape["gc"]),
        mesh=mesh, in_specs=in_specs, out_specs=out_specs, check_vma=False,
    )
```

time: 183 us -> 49.2 us (0.27)
  the two profiles are of different devices: /device:TPU:1 before, /device:TPU:0 now
where the time goes in v1:
time: 49.2 us; the launch traced here: 49.1 us
  Pallas kernels  46.1 us (94%)
  local copies, waits for them, and re-layouts  3 us (6%)
    pallas_call x1, Pallas kernels, on_device(): pl.pallas_call(functools.partial(kernel, groups), out_shape=jax.ShapeDtyp...  46.1 us
    unnamed x3, local copies, waits for them, and re-layouts  3 us

profile of v1, /device:TPU:0, one launch (start us, length us, event | category | flops | bytes accessed | tf_op | source)
XLA Modules:
  0.0 49.1 jit_solution(2163873618345339175)
XLA Ops:
  0.0 0.0 copy-start
  0.0 1.6 %copy-done = f32[1,8,256,256]{3,2,1,0:T(8,128)S(1)} copy-done((f32[1,8,256,256]{3,2,1,0:T(8,128)S(1)}, f32[1,8,256,256]{3,2,1,0:T(8,128)}, u32[]{:S(2)}) %copy-start) | copy-done | bytes 2097176
  1.6 46.1 %shard_map.17 = f32[8,192,384]{2,1,0:T(8,128)S(1)} custom-call(f32[8,256,256]{2,1,0:T(8,128)S(1)} %bitcast.3), custom_call_target="tpu_custom_call" | custom-call | tf_op jit(solution)/shard_map/pallas_call | solution.py:285
  47.7 1.4 %copy.3 = f32[1,8,192,384]{3,2,1,0:T(8,128)} copy(f32[1,8,192,384]{3,2,1,0:T(8,128)S(1)} %bitcast.2) | data formatting | bytes 4718592
Async XLA Ops:
  0.0 1.6 %copy-start = (f32[1,8,256,256]{3,2,1,0:T(8,128)S(1)}, f32[1,8,256,256]{3,2,1,0:T(8,128)}, u32[]{:S(2)}) copy-start(f32[1,8,256,256]{3,2,1,0:T(8,128)} %param.1) | copy-start | bytes 6291460

commit v2 on v1

v2 whole, which is shorter than its diff:
```python
import functools

import jax
import jax.numpy as jnp
from jax import lax
from jax.experimental import pallas as pl
from jax.experimental.pallas import tpu as pltpu
from jax.sharding import PartitionSpec as P

EXTERIOR = 768
NEWTON = 4
MESH = pl.DeviceIdType.MESH
CHUNKS = 4


def dot32(left, right):
    return jnp.dot(
        left, right, precision=lax.Precision.HIGHEST, preferred_element_type=jnp.float32
    )


def halves(x):
    high = x.astype(jnp.bfloat16)
    return high, (x - high.astype(jnp.float32)).astype(jnp.bfloat16)


def dot3(left, right):
    lh, ll = halves(left)
    rh, rl = halves(right)
    dot = functools.partial(jnp.dot, preferred_element_type=jnp.float32)
    return dot(lh, rh) + (dot(lh, rl) + dot(ll, rh))


def kernel(
    groups, hbm_ref, out_ref, x_ref, rows, strips, ei, ie, inv, wall, load,
    row_send, row_recv, strip_send, strip_recv, ei_send, ei_recv,
    ie_send, ie_recv, inv_send, inv_recv,
):
    merges, block, _ = x_ref.shape
    ext = EXTERIOR // 4
    num = block - ext
    half_ext = ext // 2
    half_num = num // 2
    wide = ext - num
    per = merges // CHUNKS
    tile = lax.axis_index("tile")
    gr = lax.axis_index("gr")
    gc = lax.axis_index("gc")
    side = tile % 2
    core = gr % 2
    pos = gr // 2
    me = side * 4 + gr

    staged = pltpu.make_async_copy(hbm_ref, x_ref, load)
    staged.start()

    def across(j):
        far_side = 1 - side if j & 4 else side
        far_pos = 1 - pos if j & 2 else pos
        far_core = 1 - core if j & 1 else core
        device = {"tile": tile - side + far_side, "gr": far_pos * 2 + far_core}
        return device, far_side * 4 + far_pos * 2 + far_core

    barrier = pltpu.get_barrier_semaphore()
    for j in range(1, 8):
        pl.semaphore_signal(barrier, inc=1, device_id=across(j)[0], device_id_type=MESH)
    for d in range(1, groups):
        pl.semaphore_signal(
            barrier, inc=1, device_id={"gc": (gc + d) % groups}, device_id_type=MESH
        )
    pl.semaphore_wait(barrier, 7 + groups - 1)
    staged.wait()

    def row_copy(j):
        device, other = across(j)
        return pltpu.make_async_remote_copy(
            src_ref=x_ref.at[other, pl.ds(ext, num), pl.ds(wide, 2 * num)],
            dst_ref=rows.at[me],
            send_sem=row_send.at[j - 1],
            recv_sem=row_recv.at[j - 1],
            device_id=device,
            device_id_type=MESH,
        )

    def gather_moves(buf, send_sems, recv_sems):
        size = buf.shape[1] // 2

        def move(index, owner, half, j):
            part = pl.ds(half * size, size)
            return pltpu.make_async_remote_copy(
                src_ref=buf.at[owner, part],
                dst_ref=buf.at[owner, part],
                send_sem=send_sems.at[index],
                recv_sem=recv_sems.at[index],
                device_id=across(j)[0],
                device_id_type=MESH,
            )

        far = {j: across(j)[1] for j in (2, 4, 6)}
        moves = {}
        index = 0
        for half in range(2):
            for j in (4, 2, 1):
                moves["own", half, j] = move(index, me, half, j)
                index += 1
            for j in (4, 2, 6):
                moves["pass", half, j] = move(index, far[j], half, 1)
                index += 1
        moves["turn", 1, 4] = move(index, far[4], 1, 2)
        moves["turn", 0, 2] = move(index + 1, far[2], 0, 4)
        return moves

    def send_own(moves):
        for half, j in ((1, 4), (0, 2), (0, 4), (1, 2), (1, 1), (0, 1)):
            moves["own", half, j].start()

    def send_turns(moves):
        for half, j in ((1, 4), (0, 2)):
            moves["own", half, j].wait_recv()
            moves["turn", half, j].start()
            moves["pass", half, j].start()

    def send_rest(moves):
        for half, j in ((0, 4), (1, 2)):
            moves["own", half, j].wait_recv()
            moves["pass", half, j].start()

    def send_diagonal(moves):
        for half, j in ((1, 4), (0, 2)):
            moves["turn", half, j].wait_recv()
            moves["pass", half, 6].start()

    def get_rest(moves):
        for half in range(2):
            moves["own", half, 1].wait_recv()
            for j in (4, 2, 6):
                moves["pass", half, j].wait_recv()

    def ei_copy(way, d, k):
        source = gc - d if way == 0 else gc + d
        part = pl.ds(k * per, per)
        return pltpu.make_async_remote_copy(
            src_ref=ei.at[source, part],
            dst_ref=ei.at[source, part],
            send_sem=ei_send.at[way, d, k],
            recv_sem=ei_recv.at[way, d, k],
            device_id={"gc": gc + 1 if way == 0 else gc - 1},
            device_id_type=MESH,
        )

    def sends(way, d):
        if way == 0:
            return jnp.logical_and(gc < groups - 1, gc >= d)
        return jnp.logical_and(gc > 0, gc + d < groups)

    def gets(way, d):
        return gc - 1 - d >= 0 if way == 0 else gc + 1 + d < groups

    def ei_start(d, k):
        for way in range(2):
            @pl.when(sends(way, d))
            def _():
                ei_copy(way, d, k).start()

    def ei_get(d, k):
        for way in range(2):
            @pl.when(gets(way, d))
            def _():
                ei_copy(way, d, k).wait_recv()

    for j in range(1, 8):
        row_copy(j).start()
    rows[me] = x_ref[me, ext:, wide:]

    def pack_ei(m, carry):
        ei[gc, m] = jnp.concatenate(
            [x_ref[m, :half_ext, ext:], x_ref[m, half_ext:ext, ext:]], axis=1
        )
        return carry

    def pack_ie(m, carry):
        ie[me, m, :num] = x_ref[m, ext:, :wide]
        ie[me, m, num:] = jnp.concatenate(
            [x_ref[m, ext : ext + half_num, wide:ext], x_ref[m, ext + half_num :, wide:ext]],
            axis=1,
        )
        return carry

    lax.fori_loop(0, merges, pack_ei, 0)
    for k in range(CHUNKS // 2):
        ei_start(0, k)
    lax.fori_loop(0, merges, pack_ie, 0)
    ie_moves = gather_moves(ie, ie_send, ie_recv)
    inv_moves = gather_moves(inv, inv_send, inv_recv)
    send_own(ie_moves)

    for j in range(1, 8):
        row_copy(j).wait_recv()
    total = [rows[g][:, num:] + rows[4 + g][:, num:] for g in range(4)]
    left = jnp.concatenate(total[:2], axis=0)
    right = jnp.concatenate(total[2:], axis=0)
    strips[gc] = jnp.concatenate([left, right], axis=1)

    def strip_copy(d):
        return pltpu.make_async_remote_copy(
            src_ref=strips.at[gc],
            dst_ref=strips.at[gc],
            send_sem=strip_send.at[d - 1],
            recv_sem=strip_recv.at[d - 1],
            device_id={"gc": (gc + d) % groups},
            device_id_type=MESH,
        )

    for d in range(1, groups):
        strip_copy(d).start()
    for k in range(CHUNKS // 2, CHUNKS):
        ei_start(0, k)
    for k in range(CHUNKS // 2):
        ei_get(0, k)
        ei_start(1, k)
    send_turns(ie_moves)

    for d in range(1, groups):
        strip_copy(d).wait_recv()
    interface = jnp.concatenate(
        [
            jnp.concatenate([strips[g][:, :num] for g in range(groups)], axis=1),
            jnp.concatenate([strips[g][:, num:] for g in range(groups)], axis=1),
        ],
        axis=0,
    )
    eye = lax.broadcasted_iota(jnp.int32, interface.shape, 0) == lax.broadcasted_iota(
        jnp.int32, interface.shape, 1
    )
    largest = jnp.max(jnp.where(eye, interface, -jnp.inf), axis=(0, 1), keepdims=True)
    scale = 1.0 / largest
    inverse = jnp.where(eye, 2.0 * scale, 0.0) - (interface * scale) * scale
    for step in range(NEWTON - 1):
        inverse = 2.0 * inverse - dot32(dot32(inverse, interface), inverse)
    inv[me] = inverse
    send_own(inv_moves)

    for k in range(CHUNKS // 2, CHUNKS):
        ei_get(0, k)
        ei_start(1, k)
    send_rest(ie_moves)
    send_diagonal(ie_moves)
    for k in range(CHUNKS // 2):
        ei_get(1, k)
        ei_start(2, k)
    send_turns(inv_moves)
    for k in range(CHUNKS // 2, CHUNKS):
        ei_get(1, k)
        ei_start(2, k)
    send_rest(inv_moves)
    send_diagonal(inv_moves)
    get_rest(ie_moves)
    get_rest(inv_moves)

    def solve(m, carry):
        for g in range(4):
            parts = []
            for s in range(2):
                parts.append(ie[s * 4 + g, m, :num])
                parts.append(
                    jnp.concatenate(
                        [ie[s * 4 + g, m, num:, :num], ie[s * 4 + g, m, num:, num:]], axis=0
                    )
                )
            wall[m, pl.ds(g * num, num)] = jnp.concatenate(parts, axis=1)
        wall[m] = dot3(inv[m], wall[m])
        return carry

    lax.fori_loop(0, merges, solve, 0)

    def finish(m, carry):
        coupling = jnp.concatenate(
            [
                jnp.concatenate([ei[g, m][:, :num] for g in range(groups)], axis=1),
                jnp.concatenate([ei[g, m][:, num:] for g in range(groups)], axis=1),
            ],
            axis=0,
        )
        own_part = x_ref[m, :ext, :ext]
        blank = jnp.zeros_like(own_part)
        first = jnp.where(side == 0, own_part, blank)
        second = jnp.where(side == 0, blank, own_part)
        out_ref[m] = jnp.concatenate([first, second], axis=1) - dot3(coupling, wall[m])
        return carry

    for k in range(CHUNKS):
        for d in range(2, groups - 1):
            ei_get(d, k)
        lax.fori_loop(k * per, (k + 1) * per, finish, 0)

    for j in range(1, 8):
        row_copy(j).wait_send()
    for d in range(1, groups):
        strip_copy(d).wait_send()
    for way in range(2):
        for d in range(groups - 1):
            @pl.when(sends(way, d))
            def _():
                for k in range(CHUNKS):
                    ei_copy(way, d, k).wait_send()
    for move in (*ie_moves.values(), *inv_moves.values()):
        move.wait_send()


def on_device(groups, child_maps):
    blocks = child_maps[0]
    merges, block, _ = blocks.shape
    ext = EXTERIOR // 4
    num = block - ext
    dma = pltpu.SemaphoreType.DMA
    f32 = jnp.float32
    merged = pl.pallas_call(
        functools.partial(kernel, groups),
        out_shape=jax.ShapeDtypeStruct((merges, ext, 2 * ext), f32),
        in_specs=[pl.BlockSpec(memory_space=pltpu.HBM)],
        out_specs=pl.BlockSpec(memory_space=pltpu.VMEM),
        scratch_shapes=[
            pltpu.VMEM((merges, block, block), f32),
            pltpu.VMEM((merges, num, 2 * num), f32),
            pltpu.VMEM((groups, 2 * num, 2 * num), f32),
            pltpu.VMEM((groups, merges, ext // 2, 2 * num), f32),
            pltpu.VMEM((merges, merges, num + num // 2, 2 * num), f32),
            pltpu.VMEM((merges, 4 * num, 4 * num), f32),
            pltpu.VMEM((merges, 4 * num, 2 * ext), f32),
            dma,
            dma((7,)),
            dma((7,)),
            dma((groups - 1,)),
            dma((groups - 1,)),
            dma((2, groups - 1, CHUNKS)),
            dma((2, groups - 1, CHUNKS)),
            dma((14,)),
            dma((14,)),
            dma((14,)),
            dma((14,)),
        ],
        compiler_params=pltpu.CompilerParams(
            collective_id=0, has_side_effects=True, vmem_limit_bytes=48 * 1024 * 1024
        ),
    )(blocks)
    return merged[None]


def solution(mesh):
    in_specs = (P("tile", None, "gr", "gc"),)
    out_specs = P("tile", None, "gr", "gc")
    return jax.shard_map(
        functools.partial(on_device, mesh.shape["gc"]),
        mesh=mesh, in_specs=in_specs, out_specs=out_specs, check_vma=False,
    )
```

time: 49.2 us -> 44 us (0.89)
  the two profiles are of different devices: /device:TPU:0 before, /device:TPU:1 now
where the time goes in v2:
time: 44 us; the launch traced here: 43.8 us
  Pallas kernels  40.8 us (93%)
  local copies, waits for them, and re-layouts  3 us (7%)
    pallas_call x1, Pallas kernels, on_device(): pl.pallas_call(functools.partial(kernel, groups), out_shape=jax.ShapeDtyp...  40.8 us
    unnamed x3, local copies, waits for them, and re-layouts  3 us

profile of v2, /device:TPU:1, one launch (start us, length us, event | category | flops | bytes accessed | tf_op | source)
XLA Modules:
  0.0 43.8 jit_solution(2307838311912861521)
XLA Ops:
  0.0 0.0 copy-start
  0.0 1.6 %copy-done = f32[1,8,256,256]{3,2,1,0:T(8,128)S(1)} copy-done((f32[1,8,256,256]{3,2,1,0:T(8,128)S(1)}, f32[1,8,256,256]{3,2,1,0:T(8,128)}, u32[]{:S(2)}) %copy-start) | copy-done | bytes 2097176
  1.6 40.8 %shard_map.17 = f32[8,192,384]{2,1,0:T(8,128)S(1)} custom-call(f32[8,256,256]{2,1,0:T(8,128)S(1)} %bitcast.3), custom_call_target="tpu_custom_call" | custom-call | tf_op jit(solution)/shard_map/pallas_call | solution.py:317
  42.4 1.4 %copy.3 = f32[1,8,192,384]{3,2,1,0:T(8,128)} copy(f32[1,8,192,384]{3,2,1,0:T(8,128)S(1)} %bitcast.2) | data formatting | bytes 4718592
Async XLA Ops:
  0.0 1.6 %copy-start = (f32[1,8,256,256]{3,2,1,0:T(8,128)S(1)}, f32[1,8,256,256]{3,2,1,0:T(8,128)}, u32[]{:S(2)}) copy-start(f32[1,8,256,256]{3,2,1,0:T(8,128)} %param.1) | copy-start | bytes 6291460

commit v3 on v2

--- a/solution.py
+++ b/solution.py
@@ -32,7 +32,7 @@
 
 
 def kernel(
-    groups, hbm_ref, out_ref, x_ref, rows, strips, ei, ie, inv, wall, load,
+    groups, hbm_ref, out_ref, x_ref, ii, rows, strips, ei, ie, inv, wall, load,
     row_send, row_recv, strip_send, strip_recv, ei_send, ei_recv,
     ie_send, ie_recv, inv_send, inv_recv,
 ):
@@ -74,7 +74,7 @@
     def row_copy(j):
         device, other = across(j)
         return pltpu.make_async_remote_copy(
-            src_ref=x_ref.at[other, pl.ds(ext, num), pl.ds(wide, 2 * num)],
+            src_ref=ii.at[other],
             dst_ref=rows.at[me],
             send_sem=row_send.at[j - 1],
             recv_sem=row_recv.at[j - 1],
@@ -168,9 +168,13 @@
             def _():
                 ei_copy(way, d, k).wait_recv()
 
-    for j in range(1, 8):
+    for m in range(merges):
+        ii[m] = jnp.concatenate(
+            [x_ref[m, ext : ext + half_num, ext:], x_ref[m, ext + half_num :, ext:]], axis=1
+        )
+    for j in (6, 7, 4, 5, 2, 3, 1):
         row_copy(j).start()
-    rows[me] = x_ref[me, ext:, wide:]
+    rows[me] = ii[me]
 
     def pack_ei(m, carry):
         ei[gc, m] = jnp.concatenate(
@@ -196,9 +200,10 @@
 
     for j in range(1, 8):
         row_copy(j).wait_recv()
-    total = [rows[g][:, num:] + rows[4 + g][:, num:] for g in range(4)]
-    left = jnp.concatenate(total[:2], axis=0)
-    right = jnp.concatenate(total[2:], axis=0)
+    total = [rows[g] + rows[4 + g] for g in range(4)]
+    total = [part for pair in total for part in (pair[:, :num], pair[:, num:])]
+    left = jnp.concatenate(total[:4], axis=0)
+    right = jnp.concatenate(total[4:], axis=0)
     strips[gc] = jnp.concatenate([left, right], axis=1)
 
     def strip_copy(d):
@@ -321,7 +326,8 @@
         out_specs=pl.BlockSpec(memory_space=pltpu.VMEM),
         scratch_shapes=[
             pltpu.VMEM((merges, block, block), f32),
-            pltpu.VMEM((merges, num, 2 * num), f32),
+            pltpu.VMEM((merges, num // 2, 2 * num), f32),
+            pltpu.VMEM((merges, num // 2, 2 * num), f32),
             pltpu.VMEM((groups, 2 * num, 2 * num), f32),
             pltpu.VMEM((groups, merges, ext // 2, 2 * num), f32),
             pltpu.VMEM((merges, merges, num + num // 2, 2 * num), f32),

time: 44 us -> 42.8 us (0.973)
  Pallas kernels: 40.8 us -> 39.6 us
    pallas_call x1, Pallas kernels: 40.8 us -> 39.6 us  [on_device(): pl.pallas_call(functools.partial(kernel, groups), out_shape=jax.ShapeDtyp...]
where the time goes in v3:
time: 42.8 us; the launch traced here: 42.7 us
  Pallas kernels  39.6 us (93%)
  local copies, waits for them, and re-layouts  3 us (7%)
    pallas_call x1, Pallas kernels, on_device(): pl.pallas_call(functools.partial(kernel, groups), out_shape=jax.ShapeDtyp...  39.6 us
    unnamed x3, local copies, waits for them, and re-layouts  3 us

profile of v3, /device:TPU:1, one launch (start us, length us, event | category | flops | bytes accessed | tf_op | source)
XLA Modules:
  0.0 42.7 jit_solution(3782575712676824405)
XLA Ops:
  0.0 0.0 copy-start
  0.0 1.6 %copy-done = f32[1,8,256,256]{3,2,1,0:T(8,128)S(1)} copy-done((f32[1,8,256,256]{3,2,1,0:T(8,128)S(1)}, f32[1,8,256,256]{3,2,1,0:T(8,128)}, u32[]{:S(2)}) %copy-start) | copy-done | bytes 2097176
  1.6 39.6 %shard_map.17 = f32[8,192,384]{2,1,0:T(8,128)S(1)} custom-call(f32[8,256,256]{2,1,0:T(8,128)S(1)} %bitcast.3), custom_call_target="tpu_custom_call" | custom-call | tf_op jit(solution)/shard_map/pallas_call | solution.py:322
  41.2 1.4 %copy.3 = f32[1,8,192,384]{3,2,1,0:T(8,128)} copy(f32[1,8,192,384]{3,2,1,0:T(8,128)S(1)} %bitcast.2) | data formatting | bytes 4718592
Async XLA Ops:
  0.0 1.6 %copy-start = (f32[1,8,256,256]{3,2,1,0:T(8,128)S(1)}, f32[1,8,256,256]{3,2,1,0:T(8,128)}, u32[]{:S(2)}) copy-start(f32[1,8,256,256]{3,2,1,0:T(8,128)} %param.1) | copy-start | bytes 6291460

commit v4 on v3

--- a/solution.py
+++ b/solution.py
@@ -68,8 +68,6 @@
         pl.semaphore_signal(
             barrier, inc=1, device_id={"gc": (gc + d) % groups}, device_id_type=MESH
         )
-    pl.semaphore_wait(barrier, 7 + groups - 1)
-    staged.wait()
 
     def row_copy(j):
         device, other = across(j)
@@ -168,12 +166,11 @@
             def _():
                 ei_copy(way, d, k).wait_recv()
 
+    staged.wait()
     for m in range(merges):
         ii[m] = jnp.concatenate(
             [x_ref[m, ext : ext + half_num, ext:], x_ref[m, ext + half_num :, ext:]], axis=1
         )
-    for j in (6, 7, 4, 5, 2, 3, 1):
-        row_copy(j).start()
     rows[me] = ii[me]
 
     def pack_ei(m, carry):
@@ -191,9 +188,12 @@
         return carry
 
     lax.fori_loop(0, merges, pack_ei, 0)
+    lax.fori_loop(0, merges, pack_ie, 0)
+    pl.semaphore_wait(barrier, 7 + groups - 1)
+    for j in (6, 7, 4, 5, 2, 3, 1):
+        row_copy(j).start()
     for k in range(CHUNKS // 2):
         ei_start(0, k)
-    lax.fori_loop(0, merges, pack_ie, 0)
     ie_moves = gather_moves(ie, ie_send, ie_recv)
     inv_moves = gather_moves(inv, inv_send, inv_recv)
     send_own(ie_moves)

time: 42.8 us -> 42.1 us (0.984)
  Pallas kernels: 39.6 us -> 39 us
    pallas_call x1, Pallas kernels: 39.6 us -> 39 us  [on_device(): pl.pallas_call(functools.partial(kernel, groups), out_shape=jax.ShapeDtyp...]
where the time goes in v4:
time: 42.1 us; the launch traced here: 42 us
  Pallas kernels  39 us (93%)
  local copies, waits for them, and re-layouts  3 us (7%)
    pallas_call x1, Pallas kernels, on_device(): pl.pallas_call(functools.partial(kernel, groups), out_shape=jax.ShapeDtyp...  39 us
    unnamed x3, local copies, waits for them, and re-layouts  3 us

profile of v4, /device:TPU:1, one launch (start us, length us, event | category | flops | bytes accessed | tf_op | source)
XLA Modules:
  0.0 42.0 jit_solution(1361318209874417642)
XLA Ops:
  0.0 0.0 copy-start
  0.0 1.6 %copy-done = f32[1,8,256,256]{3,2,1,0:T(8,128)S(1)} copy-done((f32[1,8,256,256]{3,2,1,0:T(8,128)S(1)}, f32[1,8,256,256]{3,2,1,0:T(8,128)}, u32[]{:S(2)}) %copy-start) | copy-done | bytes 2097176
  1.6 39.0 %shard_map.17 = f32[8,192,384]{2,1,0:T(8,128)S(1)} custom-call(f32[8,256,256]{2,1,0:T(8,128)S(1)} %bitcast.3), custom_call_target="tpu_custom_call" | custom-call | tf_op jit(solution)/shard_map/pallas_call | solution.py:322
  40.6 1.4 %copy.3 = f32[1,8,192,384]{3,2,1,0:T(8,128)} copy(f32[1,8,192,384]{3,2,1,0:T(8,128)S(1)} %bitcast.2) | data formatting | bytes 4718592
Async XLA Ops:
  0.0 1.6 %copy-start = (f32[1,8,256,256]{3,2,1,0:T(8,128)S(1)}, f32[1,8,256,256]{3,2,1,0:T(8,128)}, u32[]{:S(2)}) copy-start(f32[1,8,256,256]{3,2,1,0:T(8,128)} %param.1) | copy-start | bytes 6291460
